TPU v7x, 32 devices: a whole 2x2x4 slice. The times are simulated.
32 devices in a mesh: tm: 8 (over z, x), cam: 4 (over y, core).
Axes of the slice: x: 2, y: 2, z: 4, core: 2. Of those that a mesh axis runs over, the one named last changes fastest.
Arguments:
- tokens: bfloat16 [4, 8, 512, 1536], P('cam', 'tm'), may hold values from -6 to 6
- w_query: bfloat16 [1536, 768], replicated, may hold values from -18 to 18
- w_key: bfloat16 [1536, 768], replicated, may hold values from -1 to 1
- w_value: bfloat16 [1536, 768], replicated, may hold values from -0.15625 to 0.15625
- w_out: bfloat16 [768, 1536], replicated, may hold values from -1.75 to 1.75
- grad_update: bfloat16 [4, 8, 512, 1536], P('cam', 'tm'), may hold values from -6 to 6
- memory_offsets: int32 [8, 4], replicated, may hold values from 1 to 7, as said below
- strip_count: int32 [4, 4], replicated, may hold values from 0 to 2, as said below
- strip_index: int32 [4, 4, 2], replicated, may hold values from 0 to 3, as said below
Outputs:
- update: bfloat16 [4, 8, 512, 1536], P('cam', 'tm')
- grad_tokens: bfloat16 [4, 8, 512, 1536], P('cam', 'tm')
Inputs may be any that keep to these rules, and one draw needn't show every extreme that they name: `memory_offsets`: every entry of row f is at most max(f, 1). strip_count[c, c] is 0. For every camera c the sum over s of strip_count[s, c] is at most 4; it is exactly 4 for some camera, and some entry is 2. The 2 entries of strip_index[s, c] are different.
All inputs are finite; a program needn't handle non-finite values.
Results may differ from a plain program's by a relative error of at most 0.0085.
The roundings to bfloat16 on the way count: a program that leaves them out, or rounds other values in their place, can miss the bound.
Values may be sent and summed in bfloat16 or wider, within the bound.
A program may use at most 128 MiB of HBM per device.

v0:
```python
from functools import partial
import math

import jax
import jax.numpy as jnp
from jax import lax
from jax.sharding import PartitionSpec as P

HDIM = 64
STRIP = 128
MEM = 32
RMAX = 4


EPS = 1e-05
CONTRACT_LAST = (((1,), (1,)), ((), ()))


def normalize(values_in):
    widened = values_in.astype(jnp.float32)
    average = jnp.mean(widened, axis=-1, keepdims=True)
    centred = widened - average
    spread = jnp.mean(centred * centred, axis=-1, keepdims=True)
    inverse = lax.rsqrt(spread + EPS)
    return (centred * inverse, inverse)


def norm_backward(grad_normed, normed, inverse):
    first_mean = jnp.mean(grad_normed, axis=-1, keepdims=True)
    second_mean = jnp.mean(grad_normed * normed, axis=-1, keepdims=True)
    return inverse * (grad_normed - first_mean - normed * second_mean)


def group_pass(operands, key_live):
    query_grp, key_grp, value_grp, grad_grp = operands
    frames_here, row_count, group_width = query_grp.shape
    key_count = key_grp.shape[1]
    pair_count = group_width // HDIM
    score_scale = 1.0 / math.sqrt(HDIM)
    query_four = query_grp.reshape(frames_here, row_count, pair_count, HDIM)
    key_four = key_grp.reshape(frames_here, key_count, pair_count, HDIM)
    value_four = value_grp.reshape(frames_here, key_count, pair_count, HDIM)
    grad_four = grad_grp.reshape(frames_here, row_count, pair_count, HDIM)
    scores = (
        jnp.einsum("fqhd,fkhd->fhqk", query_four, key_four, preferred_element_type=jnp.float32)
        * score_scale
    )
    scores = jnp.where(key_live[:, None, None, :], scores, -jnp.inf)
    highest = jnp.max(scores, axis=-1, keepdims=True)
    shifted_exp = jnp.exp(scores - highest)
    weights = shifted_exp / jnp.sum(shifted_exp, axis=-1, keepdims=True)
    weights_low = weights.astype(jnp.bfloat16)
    mixed_rows = jnp.einsum(
        "fhqk,fkhd->fqhd", weights_low, value_four, preferred_element_type=jnp.float32
    )
    mixed_rows = mixed_rows.astype(jnp.bfloat16).reshape(frames_here, row_count, group_width)
    grad_weights = jnp.einsum(
        "fqhd,fkhd->fhqk", grad_four, value_four, preferred_element_type=jnp.float32
    )
    inner_sum = jnp.sum(weights * grad_weights, axis=-1, keepdims=True)
    grad_scores = (weights * (grad_weights - inner_sum) * score_scale).astype(jnp.bfloat16)
    grad_query = jnp.einsum(
        "fhqk,fkhd->fqhd", grad_scores, key_four, preferred_element_type=jnp.float32
    )
    grad_query = grad_query.astype(jnp.bfloat16).reshape(frames_here, row_count, group_width)
    grad_key = jnp.einsum(
        "fhqk,fqhd->fkhd", grad_scores, query_four, preferred_element_type=jnp.float32
    )
    grad_value = jnp.einsum(
        "fhqk,fqhd->fkhd", weights_low, grad_four, preferred_element_type=jnp.float32
    )
    grad_key = grad_key.reshape(frames_here, key_count, group_width)
    grad_value = grad_value.reshape(frames_here, key_count, group_width)
    return (mixed_rows, grad_query, grad_key, grad_value)


def local(
    tokens, w_query, w_key, w_value, w_out, grad_update, memory_offsets, strip_count, strip_index
):
    frames_here = tokens.shape[1]
    row_count = tokens.shape[2]
    model_width = tokens.shape[3]
    inner_width = w_query.shape[1]
    total_rows = frames_here * row_count
    normed, inverse = normalize(tokens.reshape(total_rows, model_width))
    normed_low = normed.astype(jnp.bfloat16)

    def project(weight):
        result = jnp.dot(normed_low, weight, preferred_element_type=jnp.float32)
        return result.astype(jnp.bfloat16).reshape(frames_here, row_count, inner_width)

    queries = project(w_query)
    keys_here = project(w_key)
    values_here = project(w_value)
    grad_mixed = lax.dot_general(
        grad_update.reshape(total_rows, model_width),
        w_out,
        CONTRACT_LAST,
        preferred_element_type=jnp.float32,
    )
    grad_mixed = grad_mixed.astype(jnp.bfloat16).reshape(frames_here, row_count, inner_width)
    spacing = row_count // MEM
    kept_keys = keys_here.reshape(frames_here, MEM, spacing, inner_width)[:, :, 0]
    kept_values = values_here.reshape(frames_here, MEM, spacing, inner_width)[:, :, 0]
    all_keys, all_values = (
        lax.all_gather(kept_keys, "tm", axis=0, tiled=True),
        lax.all_gather(kept_values, "tm", axis=0, tiled=True),
    )
    frame_total = all_keys.shape[0]
    first_frame = lax.axis_index("tm") * frames_here
    frame_ids = first_frame + jnp.arange(frames_here, dtype=jnp.int32)
    offsets_here = jnp.take(memory_offsets, frame_ids, axis=0)
    read_count = offsets_here.shape[1]
    sources = frame_ids[:, None] - offsets_here
    source_live = sources >= 0
    source_safe = jnp.maximum(sources, 0)
    memory_rows = read_count * MEM
    memory_keys = jnp.take(all_keys, source_safe.reshape(-1), axis=0).reshape(
        frames_here, memory_rows, inner_width
    )
    memory_values = jnp.take(all_values, source_safe.reshape(-1), axis=0).reshape(
        frames_here, memory_rows, inner_width
    )
    memory_live = jnp.repeat(source_live, MEM, axis=1)
    camera = lax.axis_index("cam")
    camera_count = lax.axis_size("cam")
    slots_max = strip_index.shape[2]
    slot_total = camera_count * slots_max
    strips_frame = row_count // STRIP
    sent_index = lax.dynamic_index_in_dim(strip_index, camera, 0, keepdims=False)
    sent_count = lax.dynamic_index_in_dim(strip_count, camera, 0, keepdims=False)
    received_count = lax.dynamic_index_in_dim(strip_count, camera, 1, keepdims=False)
    key_strips = keys_here.reshape(frames_here, strips_frame, STRIP, inner_width)
    value_strips = values_here.reshape(frames_here, strips_frame, STRIP, inner_width)
    sent_keys = jnp.take(key_strips, sent_index.reshape(-1), axis=1)
    sent_values = jnp.take(value_strips, sent_index.reshape(-1), axis=1)
    sent_keys = sent_keys.reshape(frames_here, camera_count, slots_max, STRIP, inner_width)
    sent_values = sent_values.reshape(frames_here, camera_count, slots_max, STRIP, inner_width)
    got_keys, got_values = (
        lax.all_to_all(sent_keys, "cam", split_axis=1, concat_axis=1, tiled=True),
        lax.all_to_all(sent_values, "cam", split_axis=1, concat_axis=1, tiled=True),
    )
    slot_ids = jnp.arange(slots_max, dtype=jnp.int32)
    got_live = (slot_ids[None, :] < received_count[:, None]).reshape(-1)
    got_keys = got_keys.reshape(frames_here, slot_total, STRIP * inner_width)
    got_values = got_values.reshape(frames_here, slot_total, STRIP * inner_width)
    position = jnp.cumsum(got_live.astype(jnp.int32), dtype=jnp.int32) - 1
    packed_ids = jnp.arange(RMAX, dtype=jnp.int32)
    picker = jnp.logical_and(position[None, :] == packed_ids[:, None], got_live[None, :])
    picker_low = picker.astype(jnp.bfloat16)
    far_keys = jnp.einsum("rs,fsn->frn", picker_low, got_keys, preferred_element_type=jnp.float32)
    far_values = jnp.einsum(
        "rs,fsn->frn", picker_low, got_values, preferred_element_type=jnp.float32
    )
    far_keys = far_keys.astype(jnp.bfloat16).reshape(frames_here, RMAX * STRIP, inner_width)
    far_values = far_values.astype(jnp.bfloat16).reshape(frames_here, RMAX * STRIP, inner_width)
    live_total = jnp.sum(got_live.astype(jnp.int32))
    far_live = jnp.repeat(packed_ids < live_total, STRIP)
    key_rows = jnp.concatenate([keys_here, memory_keys, far_keys], axis=1)
    value_rows = jnp.concatenate([values_here, memory_values, far_values], axis=1)
    key_live = jnp.concatenate(
        [jnp.ones((frames_here, row_count), dtype=bool), memory_live, far_live[None, :]], axis=1
    )
    group_width = 2 * HDIM
    group_count = inner_width // group_width

    def split_groups(array):
        shaped = array.reshape(array.shape[0], array.shape[1], group_count, group_width)
        return jnp.moveaxis(shaped, 2, 0)

    def join_groups(array):
        return jnp.moveaxis(array, 0, 2).reshape(array.shape[1], array.shape[2], inner_width)

    results = lax.map(
        partial(group_pass, key_live=key_live),
        (
            split_groups(queries),
            split_groups(key_rows),
            split_groups(value_rows),
            split_groups(grad_mixed),
        ),
    )
    mixed_rows, grad_query, grad_keys_all, grad_values_all = [
        join_groups(result_part) for result_part in results
    ]
    update = jnp.dot(
        mixed_rows.reshape(total_rows, inner_width), w_out, preferred_element_type=jnp.float32
    )
    update = update.astype(jnp.bfloat16).reshape(1, frames_here, row_count, model_width)
    split_at = row_count + memory_rows
    memory_stack = jnp.stack(
        [
            grad_keys_all[:, row_count:split_at].reshape(frames_here, read_count, MEM, inner_width),
            grad_values_all[:, row_count:split_at].reshape(
                frames_here, read_count, MEM, inner_width
            ),
        ],
        axis=2,
    )
    flat_stack = memory_stack.reshape(frames_here * read_count, 2, MEM, inner_width)
    flat_source = source_safe.reshape(-1)
    flat_live = source_live.reshape(-1)
    targets = jnp.arange(frame_total, dtype=jnp.int32)
    total = jnp.zeros((frame_total, 2, MEM, inner_width), jnp.float32)
    for read_at in range(frames_here * read_count):
        hit = jnp.logical_and(targets == flat_source[read_at], flat_live[read_at])
        total = total + jnp.where(hit[:, None, None, None], flat_stack[read_at][None], 0.0)
    whole_grads = lax.psum(total.astype(jnp.bfloat16), "tm").astype(jnp.float32)
    kept_grads = lax.dynamic_slice_in_dim(whole_grads, first_frame, frames_here, 0)
    far_grad_keys = grad_keys_all[:, split_at:]
    far_grad_values = grad_values_all[:, split_at:]
    safe_position = jnp.maximum(position, 0)
    slot_mask = got_live[None, :, None]
    slot_grad_keys = jnp.take(
        far_grad_keys.reshape(frames_here, RMAX, STRIP * inner_width), safe_position, axis=1
    )
    slot_grad_values = jnp.take(
        far_grad_values.reshape(frames_here, RMAX, STRIP * inner_width), safe_position, axis=1
    )
    slot_grad_keys = jnp.where(slot_mask, slot_grad_keys, 0.0)
    slot_grad_values = jnp.where(slot_mask, slot_grad_values, 0.0)
    back_keys = slot_grad_keys.astype(jnp.bfloat16).reshape(
        frames_here, camera_count, slots_max, STRIP, inner_width
    )
    back_values = slot_grad_values.astype(jnp.bfloat16).reshape(
        frames_here, camera_count, slots_max, STRIP, inner_width
    )
    returned_keys, returned_values = (
        lax.all_to_all(back_keys, "cam", split_axis=1, concat_axis=1, tiled=True),
        lax.all_to_all(back_values, "cam", split_axis=1, concat_axis=1, tiled=True),
    )
    sent_live = (slot_ids[None, :] < sent_count[:, None]).reshape(-1)
    strip_ids = jnp.arange(strips_frame, dtype=jnp.int32)
    placer = jnp.logical_and(
        sent_index.reshape(-1)[:, None] == strip_ids[None, :], sent_live[:, None]
    )
    placer = placer.astype(jnp.bfloat16)
    strip_key_add = jnp.einsum(
        "sn,fsx->fnx",
        placer,
        returned_keys.reshape(frames_here, slot_total, STRIP * inner_width),
        preferred_element_type=jnp.float32,
    ).reshape(frames_here, row_count, inner_width)
    strip_value_add = jnp.einsum(
        "sn,fsx->fnx",
        placer,
        returned_values.reshape(frames_here, slot_total, STRIP * inner_width),
        preferred_element_type=jnp.float32,
    ).reshape(frames_here, row_count, inner_width)
    own_keys_grid = grad_keys_all[:, :row_count].reshape(frames_here, MEM, spacing, inner_width)
    own_keys_grid = own_keys_grid.at[:, :, 0].add(kept_grads[:, 0])
    own_values_grid = grad_values_all[:, :row_count].reshape(frames_here, MEM, spacing, inner_width)
    own_values_grid = own_values_grid.at[:, :, 0].add(kept_grads[:, 1])
    total_keys = (
        own_keys_grid.reshape(frames_here, row_count, inner_width) + strip_key_add
    ).astype(jnp.bfloat16)
    total_values = (
        own_values_grid.reshape(frames_here, row_count, inner_width) + strip_value_add
    ).astype(jnp.bfloat16)
    grad_normed = lax.dot_general(
        grad_query.reshape(total_rows, inner_width),
        w_query,
        CONTRACT_LAST,
        preferred_element_type=jnp.float32,
    )
    grad_normed = grad_normed + lax.dot_general(
        total_keys.reshape(total_rows, inner_width),
        w_key,
        CONTRACT_LAST,
        preferred_element_type=jnp.float32,
    )
    grad_normed = grad_normed + lax.dot_general(
        total_values.reshape(total_rows, inner_width),
        w_value,
        CONTRACT_LAST,
        preferred_element_type=jnp.float32,
    )
    grad_tokens = norm_backward(grad_normed, normed, inverse).astype(jnp.bfloat16)
    grad_tokens = grad_tokens.reshape(1, frames_here, row_count, model_width)
    return (update, grad_tokens)


def solution(mesh):
    in_specs = (
        P("cam", "tm", None, None),
        P(),
        P(),
        P(),
        P(),
        P("cam", "tm", None, None),
        P(),
        P(),
        P(),
    )
    out_specs = (P("cam", "tm", None, None), P("cam", "tm", None, None))
    return jax.shard_map(local, mesh=mesh, in_specs=in_specs, out_specs=out_specs, check_vma=False)
```

profile of v0, /device:TPU:0, one launch (start us, length us, event | category | flops | bytes accessed | tf_op | source)
XLA Modules:
  0.0 581.5 jit_solution(4811744304640949535)
XLA Ops:
  12.8 4.0 convolution_convert_fusion.3
  23.0 3.9 bitcast_select_fusion.2
  26.8 4.5 all-to-all-start
  40.4 33.0 %all-gather.1 = bf16[8,32,1,768]{3,1,2,0:T(8,128)(2,1)S(1)} all-gather(bf16[1,32,1,768]{3,1,2,0:T(8,128)(2,1)S(1)} %copy.103), channel_id=3, replica_groups=mesh['tm'=8,'cam'=4] {'tm'}, dimensions={0}, use_global_device_ids=true | all-gather | bytes 442368 | tf_op jit(solution)/shard_map/all_gather | solution.py:106
  75.4 30.9 %all-gather = bf16[8,32,1,768]{3,1,2,0:T(8,128)(2,1)S(1)} all-gather(bf16[1,32,1,768]{3,1,2,0:T(8,128)(2,1)S(1)} %copy.102), channel_id=2, replica_groups=mesh['tm'=8,'cam'=4] {'tm'}, dimensions={0}, use_global_device_ids=true | all-gather | bytes 442368 | tf_op jit(solution)/shard_map/all_gather | solution.py:107
  115.6 4.5 all-to-all-start.1
  133.3 6.9 %all-to-all-done.1 = bf16[1,4,2,128,768]{4,3,2,0,1:T(8,128)(2,1)} async-done(((bf16[1,4,2,128,768]{4,3,2,0,1:T(8,128)(2,1)}), bf16[1,4,2,128,768]{4,3,2,0,1:T(8,128)(2,1)}, u32[]{:S(2)}, u32[]{:S(2)}) %all-to-all-start.1) | async-done | bytes 1572896 | tf_op jit(solution)/shard_map/all_to_all | solution.py:140
  156.6 258.7 %while.19 = (s32[]{:T(128)}, bf16[6,1,512,128]{2,3,1,0:T(8,128)(2,1)}, bf16[6,1,512,128]{2,3,1,0:T(8,128)(2,1)}, f32[6,1,1152,128]{2,3,1,0:T(8,128)}, f32[6,1,11...) while((s32[]{:T(128)}, ...), condition=%wide.region_8.11_spmd, body=%wide.region_4.10_spmd.sunk | while | flops 1241130624 | bytes 39151464 | solution.py:174
  163.8 3.8 exponential_reduce_fusion.2
  170.1 12.6 %fusion.170 = bf16[2,64,512]{2,1,0:T(8,128)(2,1)} fusion(bf16[1152,2,64]{0,2,1:T(8,128)(2,1)S(1)} %bitcast.311, f32[2,512,1152]{2,1,0:T(8,128)} %fusion.169, f32[2,512,1152]{2,1,0:T(8,128)} %get-tuple-element.257, f32[2,512]{1,0:T(2,128)S(1)} %get-tuple-element.258), kind=kOutput, calls=%fused_computation.28.clone.1 | convolution fusion | flops 159320192 | bytes 9867264 | tf_op jit(solution)/shard_map/while/body/eval_jaxpr/fhqk,fkhd->fqhd/dot_general | solution.py:62
  182.7 11.4 %fusion.173 = f32[2,64,1152]{2,1,0:T(8,128)S(1)} fusion(bf16[512,2,64]{0,2,1:T(8,128)(2,1)S(1)} %bitcast.331, f32[2,512,1152]{2,1,0:T(8,128)} %fusion.169, f32[2,512,1152]{2,1,0:T(8,128)} %get-tuple-element.257, f32[2,512]{1,0:T(2,128)S(1)} %get-tuple-element.258), kind=kOutput, calls=%fused_computation.19.clone.1 | convolution fusion | flops 159254656 | bytes 10162176 | tf_op jit(solution)/shard_map/while/body/eval_jaxpr/fhqk,fqhd->fkhd/dot_general | solution.py:66
  206.9 3.8 exponential_reduce_fusion.2
  213.1 12.6 %fusion.170 = bf16[2,64,512]{2,1,0:T(8,128)(2,1)} fusion(bf16[1152,2,64]{0,2,1:T(8,128)(2,1)S(1)} %bitcast.311, f32[2,512,1152]{2,1,0:T(8,128)} %fusion.169, f32[2,512,1152]{2,1,0:T(8,128)} %get-tuple-element.257, f32[2,512]{1,0:T(2,128)S(1)} %get-tuple-element.258), kind=kOutput, calls=%fused_computation.28.clone.1 | convolution fusion | flops 159320192 | bytes 9867264 | tf_op jit(solution)/shard_map/while/body/eval_jaxpr/fhqk,fkhd->fqhd/dot_general | solution.py:62
  225.7 11.4 %fusion.173 = f32[2,64,1152]{2,1,0:T(8,128)S(1)} fusion(bf16[512,2,64]{0,2,1:T(8,128)(2,1)S(1)} %bitcast.331, f32[2,512,1152]{2,1,0:T(8,128)} %fusion.169, f32[2,512,1152]{2,1,0:T(8,128)} %get-tuple-element.257, f32[2,512]{1,0:T(2,128)S(1)} %get-tuple-element.258), kind=kOutput, calls=%fused_computation.19.clone.1 | convolution fusion | flops 159254656 | bytes 10162176 | tf_op jit(solution)/shard_map/while/body/eval_jaxpr/fhqk,fqhd->fkhd/dot_general | solution.py:66
  249.9 3.7 exponential_reduce_fusion.2
  256.1 12.6 %fusion.170 = bf16[2,64,512]{2,1,0:T(8,128)(2,1)} fusion(bf16[1152,2,64]{0,2,1:T(8,128)(2,1)S(1)} %bitcast.311, f32[2,512,1152]{2,1,0:T(8,128)} %fusion.169, f32[2,512,1152]{2,1,0:T(8,128)} %get-tuple-element.257, f32[2,512]{1,0:T(2,128)S(1)} %get-tuple-element.258), kind=kOutput, calls=%fused_computation.28.clone.1 | convolution fusion | flops 159320192 | bytes 9867264 | tf_op jit(solution)/shard_map/while/body/eval_jaxpr/fhqk,fkhd->fqhd/dot_general | solution.py:62
  268.7 11.4 %fusion.173 = f32[2,64,1152]{2,1,0:T(8,128)S(1)} fusion(bf16[512,2,64]{0,2,1:T(8,128)(2,1)S(1)} %bitcast.331, f32[2,512,1152]{2,1,0:T(8,128)} %fusion.169, f32[2,512,1152]{2,1,0:T(8,128)} %get-tuple-element.257, f32[2,512]{1,0:T(2,128)S(1)} %get-tuple-element.258), kind=kOutput, calls=%fused_computation.19.clone.1 | convolution fusion | flops 159254656 | bytes 10162176 | tf_op jit(solution)/shard_map/while/body/eval_jaxpr/fhqk,fqhd->fkhd/dot_general | solution.py:66
  292.9 3.8 exponential_reduce_fusion.2
  299.1 12.6 %fusion.170 = bf16[2,64,512]{2,1,0:T(8,128)(2,1)} fusion(bf16[1152,2,64]{0,2,1:T(8,128)(2,1)S(1)} %bitcast.311, f32[2,512,1152]{2,1,0:T(8,128)} %fusion.169, f32[2,512,1152]{2,1,0:T(8,128)} %get-tuple-element.257, f32[2,512]{1,0:T(2,128)S(1)} %get-tuple-element.258), kind=kOutput, calls=%fused_computation.28.clone.1 | convolution fusion | flops 159320192 | bytes 9867264 | tf_op jit(solution)/shard_map/while/body/eval_jaxpr/fhqk,fkhd->fqhd/dot_general | solution.py:62
  311.7 11.4 %fusion.173 = f32[2,64,1152]{2,1,0:T(8,128)S(1)} fusion(bf16[512,2,64]{0,2,1:T(8,128)(2,1)S(1)} %bitcast.331, f32[2,512,1152]{2,1,0:T(8,128)} %fusion.169, f32[2,512,1152]{2,1,0:T(8,128)} %get-tuple-element.257, f32[2,512]{1,0:T(2,128)S(1)} %get-tuple-element.258), kind=kOutput, calls=%fused_computation.19.clone.1 | convolution fusion | flops 159254656 | bytes 10162176 | tf_op jit(solution)/shard_map/while/body/eval_jaxpr/fhqk,fqhd->fkhd/dot_general | solution.py:66
  335.9 3.8 exponential_reduce_fusion.2
  342.1 12.6 %fusion.170 = bf16[2,64,512]{2,1,0:T(8,128)(2,1)} fusion(bf16[1152,2,64]{0,2,1:T(8,128)(2,1)S(1)} %bitcast.311, f32[2,512,1152]{2,1,0:T(8,128)} %fusion.169, f32[2,512,1152]{2,1,0:T(8,128)} %get-tuple-element.257, f32[2,512]{1,0:T(2,128)S(1)} %get-tuple-element.258), kind=kOutput, calls=%fused_computation.28.clone.1 | convolution fusion | flops 159320192 | bytes 9867264 | tf_op jit(solution)/shard_map/while/body/eval_jaxpr/fhqk,fkhd->fqhd/dot_general | solution.py:62
  354.7 11.4 %fusion.173 = f32[2,64,1152]{2,1,0:T(8,128)S(1)} fusion(bf16[512,2,64]{0,2,1:T(8,128)(2,1)S(1)} %bitcast.331, f32[2,512,1152]{2,1,0:T(8,128)} %fusion.169, f32[2,512,1152]{2,1,0:T(8,128)} %get-tuple-element.257, f32[2,512]{1,0:T(2,128)S(1)} %get-tuple-element.258), kind=kOutput, calls=%fused_computation.19.clone.1 | convolution fusion | flops 159254656 | bytes 10162176 | tf_op jit(solution)/shard_map/while/body/eval_jaxpr/fhqk,fqhd->fkhd/dot_general | solution.py:66
  378.9 3.8 exponential_reduce_fusion.2
  385.1 12.6 %fusion.170 = bf16[2,64,512]{2,1,0:T(8,128)(2,1)} fusion(bf16[1152,2,64]{0,2,1:T(8,128)(2,1)S(1)} %bitcast.311, f32[2,512,1152]{2,1,0:T(8,128)} %fusion.169, f32[2,512,1152]{2,1,0:T(8,128)} %get-tuple-element.257, f32[2,512]{1,0:T(2,128)S(1)} %get-tuple-element.258), kind=kOutput, calls=%fused_computation.28.clone.1 | convolution fusion | flops 159320192 | bytes 9867264 | tf_op jit(solution)/shard_map/while/body/eval_jaxpr/fhqk,fkhd->fqhd/dot_general | solution.py:62
  397.7 11.4 %fusion.173 = f32[2,64,1152]{2,1,0:T(8,128)S(1)} fusion(bf16[512,2,64]{0,2,1:T(8,128)(2,1)S(1)} %bitcast.331, f32[2,512,1152]{2,1,0:T(8,128)} %fusion.169, f32[2,512,1152]{2,1,0:T(8,128)} %get-tuple-element.257, f32[2,512]{1,0:T(2,128)S(1)} %get-tuple-element.258), kind=kOutput, calls=%fused_computation.19.clone.1 | convolution fusion | flops 159254656 | bytes 10162176 | tf_op jit(solution)/shard_map/while/body/eval_jaxpr/fhqk,fqhd->fkhd/dot_general | solution.py:66
  429.8 13.7 %gather_fusion.4 = bf16[8,98304]{1,0:T(8,128)(2,1)} fusion(bf16[4,98304]{1,0:T(4,128)(2,1)} %reshape.659, s32[1024]{0:T(1024)} %pad_clamp_fusion), kind=kCustom, calls=%fused_computation.2.clone | custom fusion | bytes 3145760 | tf_op jit(solution)/shard_map/jit(_take)/gather | solution.py:214
  443.6 3.8 fusion.50
  448.8 4.4 all-to-all-start.2
  478.9 4.7 all-to-all-start.3
  483.5 4.2 fusion.53
  487.8 49.6 %all-reduce.2.cloned.1.call-done = bf16[8,2,32,768]{3,0,2,1:T(8,128)(2,1)} async-done(((bf16[8,2,32,768]{3,0,2,1:T(8,128)(2,1)}), bf16[8,2,32,768]{3,0,2,1:T(8,128)(2,1)}) %all-reduce.2.cloned.1.call-update) | async-done | bytes 786448 | tf_op jit(solution)/shard_map/psum | solution.py:208
  (275 shorter events, 231.4 us)
Async XLA Ops:
  7.2 9.6 %copy-start = (bf16[1536,768]{1,0:T(8,128)(2,1)S(1)}, bf16[1536,768]{1,0:T(8,128)(2,1)}, u32[]{:S(2)}) copy-start(bf16[1536,768]{1,0:T(8,128)(2,1)} %param.24) | copy-start | bytes 7077892
  9.1 3.7 copy-start.18
  12.2 98.7 %copy-start.14 = (f32[512]{0:T(512)}, f32[512]{0:T(512)S(1)}, u32[]{:S(2)}) copy-start(f32[512]{0:T(512)S(1)} %broadcast_multiply_fusion.2) | copy-start | bytes 6148
  12.7 98.1 %copy-start.16 = (f32[512]{0:T(512)}, f32[512]{0:T(512)S(1)}, u32[]{:S(2)}) copy-start(f32[512]{0:T(512)S(1)} %add_rsqrt_fusion) | copy-start | bytes 6148
  26.8 5.3 copy-start.20
  26.8 88.8 %all-to-all-start = ((bf16[1,4,2,128,768]{4,3,2,0,1:T(8,128)(2,1)}), bf16[1,4,2,128,768]{4,3,2,0,1:T(8,128)(2,1)}, u32[]{:S(2)}, u32[]{:S(2)}) async-start(bf16[1,4,2,128,768]{4,3,2,0,1:T(8,128)(2,1)} %bitcast.324), calls=%async_computation | async-start | bytes 3145728 | tf_op jit(solution)/shard_map/all_to_all | solution.py:141
  32.5 7.9 %copy-start.31 = (s32[4]{0:T(128)}, s32[4]{0:T(128)S(1)}, u32[]{:S(2)}) copy-start(s32[4]{0:T(128)S(1)} %get-tuple-element.153) | copy-start | bytes 52
  115.6 24.6 %all-to-all-start.1 = ((bf16[1,4,2,128,768]{4,3,2,0,1:T(8,128)(2,1)}), bf16[1,4,2,128,768]{4,3,2,0,1:T(8,128)(2,1)}, u32[]{:S(2)}, u32[]{:S(2)}) async-start(bf16[1,4,2,128,768]{4,3,2,0,1:T(8,128)(2,1)} %bitcast.323), calls=%async_computation.1 | async-start | bytes 3145728 | tf_op jit(solution)/shard_map/all_to_all | solution.py:140
  120.1 9.2 %copy-start.26 = (s32[8]{0:T(128)S(1)}, s32[8]{0:T(128)}, u32[]{:S(2)}) copy-start(s32[8]{0:T(128)} %get-tuple-element.183) | copy-start | bytes 100
  120.1 9.8 %copy-start.28 = (s32[8,1]{0,1:T(1,128)S(1)}, s32[8,1]{0,1:T(1,128)}, u32[]{:S(2)}) copy-start(s32[8,1]{0,1:T(1,128)} %copy-done.27) | copy-start | bytes 100
  120.2 9.7 %copy-start.21 = (pred[1,1,4,128]{3,1,2,0:T(4,128)(4,1)S(1)}, pred[1,1,4,128]{3,1,2,0:T(4,128)(4,1)}, u32[]{:S(2)}) copy-start(pred[1,1,4,128]{3,1,2,0:T(4,128)(4,1)} %copy.113) | copy-start | bytes 1540
  120.2 9.7 %copy-start.30 = (pred[1,128]{1,0:T(4,128)(4,1)S(1)}, pred[1,128]{1,0:T(4,128)(4,1)}, u32[]{:S(2)}) copy-start(pred[1,128]{1,0:T(4,128)(4,1)} %broadcast_in_dim.174) | copy-start | bytes 388
  133.3 9.3 %copy-start.22 = (pred[8]{0:T(512)(128)(4,1)S(1)}, pred[8]{0:T(512)(128)(4,1)}, u32[]{:S(2)}) copy-start(pred[8]{0:T(512)(128)(4,1)} %lt.97) | copy-start | bytes 28
  158.7 23.9 %copy-start.8 = (bf16[1,1,512,128]{2,3,1,0:T(8,128)(2,1)}, bf16[1,1,512,128]{2,3,1,0:T(8,128)(2,1)S(1)}, u32[]{:S(2)}) copy-start(bf16[1,1,512,128]{2,3,1,0:T(8,128)(2,1)S(1)} %constant_dynamic-slice_fusion.13) | copy-start | bytes 393220 | tf_op jit(solution)/shard_map/while
  159.8 10.3 %copy-start.4 = (bf16[1,1,1152,128]{2,3,1,0:T(8,128)(2,1)}, bf16[1,1,1152,128]{2,3,1,0:T(8,128)(2,1)S(1)}, u32[]{:S(2)}) copy-start(bf16[1,1,1152,128]{2,3,1,0:T(8,128)(2,1)S(1)} %constant_dynamic-slice_fusion.10) | copy-start | bytes 884740 | tf_op jit(solution)/shard_map/while
  201.8 23.9 %copy-start.8 = (bf16[1,1,512,128]{2,3,1,0:T(8,128)(2,1)}, bf16[1,1,512,128]{2,3,1,0:T(8,128)(2,1)S(1)}, u32[]{:S(2)}) copy-start(bf16[1,1,512,128]{2,3,1,0:T(8,128)(2,1)S(1)} %constant_dynamic-slice_fusion.13) | copy-start | bytes 393220 | tf_op jit(solution)/shard_map/while
  202.8 10.3 %copy-start.4 = (bf16[1,1,1152,128]{2,3,1,0:T(8,128)(2,1)}, bf16[1,1,1152,128]{2,3,1,0:T(8,128)(2,1)S(1)}, u32[]{:S(2)}) copy-start(bf16[1,1,1152,128]{2,3,1,0:T(8,128)(2,1)S(1)} %constant_dynamic-slice_fusion.10) | copy-start | bytes 884740 | tf_op jit(solution)/shard_map/while
  244.8 23.9 %copy-start.8 = (bf16[1,1,512,128]{2,3,1,0:T(8,128)(2,1)}, bf16[1,1,512,128]{2,3,1,0:T(8,128)(2,1)S(1)}, u32[]{:S(2)}) copy-start(bf16[1,1,512,128]{2,3,1,0:T(8,128)(2,1)S(1)} %constant_dynamic-slice_fusion.13) | copy-start | bytes 393220 | tf_op jit(solution)/shard_map/while
  245.8 10.3 %copy-start.4 = (bf16[1,1,1152,128]{2,3,1,0:T(8,128)(2,1)}, bf16[1,1,1152,128]{2,3,1,0:T(8,128)(2,1)S(1)}, u32[]{:S(2)}) copy-start(bf16[1,1,1152,128]{2,3,1,0:T(8,128)(2,1)S(1)} %constant_dynamic-slice_fusion.10) | copy-start | bytes 884740 | tf_op jit(solution)/shard_map/while
  287.8 23.9 %copy-start.8 = (bf16[1,1,512,128]{2,3,1,0:T(8,128)(2,1)}, bf16[1,1,512,128]{2,3,1,0:T(8,128)(2,1)S(1)}, u32[]{:S(2)}) copy-start(bf16[1,1,512,128]{2,3,1,0:T(8,128)(2,1)S(1)} %constant_dynamic-slice_fusion.13) | copy-start | bytes 393220 | tf_op jit(solution)/shard_map/while
  288.8 10.3 %copy-start.4 = (bf16[1,1,1152,128]{2,3,1,0:T(8,128)(2,1)}, bf16[1,1,1152,128]{2,3,1,0:T(8,128)(2,1)S(1)}, u32[]{:S(2)}) copy-start(bf16[1,1,1152,128]{2,3,1,0:T(8,128)(2,1)S(1)} %constant_dynamic-slice_fusion.10) | copy-start | bytes 884740 | tf_op jit(solution)/shard_map/while
  330.7 23.9 %copy-start.8 = (bf16[1,1,512,128]{2,3,1,0:T(8,128)(2,1)}, bf16[1,1,512,128]{2,3,1,0:T(8,128)(2,1)S(1)}, u32[]{:S(2)}) copy-start(bf16[1,1,512,128]{2,3,1,0:T(8,128)(2,1)S(1)} %constant_dynamic-slice_fusion.13) | copy-start | bytes 393220 | tf_op jit(solution)/shard_map/while
  331.8 10.3 %copy-start.4 = (bf16[1,1,1152,128]{2,3,1,0:T(8,128)(2,1)}, bf16[1,1,1152,128]{2,3,1,0:T(8,128)(2,1)S(1)}, u32[]{:S(2)}) copy-start(bf16[1,1,1152,128]{2,3,1,0:T(8,128)(2,1)S(1)} %constant_dynamic-slice_fusion.10) | copy-start | bytes 884740 | tf_op jit(solution)/shard_map/while
  373.8 23.9 %copy-start.8 = (bf16[1,1,512,128]{2,3,1,0:T(8,128)(2,1)}, bf16[1,1,512,128]{2,3,1,0:T(8,128)(2,1)S(1)}, u32[]{:S(2)}) copy-start(bf16[1,1,512,128]{2,3,1,0:T(8,128)(2,1)S(1)} %constant_dynamic-slice_fusion.13) | copy-start | bytes 393220 | tf_op jit(solution)/shard_map/while
  374.8 10.3 %copy-start.4 = (bf16[1,1,1152,128]{2,3,1,0:T(8,128)(2,1)}, bf16[1,1,1152,128]{2,3,1,0:T(8,128)(2,1)S(1)}, u32[]{:S(2)}) copy-start(bf16[1,1,1152,128]{2,3,1,0:T(8,128)(2,1)S(1)} %constant_dynamic-slice_fusion.10) | copy-start | bytes 884740 | tf_op jit(solution)/shard_map/while
  429.8 13.7 %copy-start.23 = (pred[8]{0:T(512)(128)(4,1)S(1)}, pred[8]{0:T(512)(128)(4,1)}, u32[]{:S(2)}) copy-start(pred[8]{0:T(512)(128)(4,1)} %lt.97) | copy-start | bytes 28
  429.8 13.7 %copy-start.29 = (pred[8]{0:T(512)(128)(4,1)S(1)}, pred[8]{0:T(512)(128)(4,1)}, u32[]{:S(2)}) copy-start(pred[8]{0:T(512)(128)(4,1)} %get-tuple-element.185) | copy-start | bytes 28
  448.8 30.1 %all-to-all-start.2 = ((bf16[1,4,2,128,768]{4,3,2,0,1:T(8,128)(2,1)}), bf16[1,4,2,128,768]{4,3,2,0,1:T(8,128)(2,1)}, u32[]{:S(2)}, u32[]{:S(2)}) async-start(bf16[1,4,2,128,768]{4,3,2,0,1:T(8,128)(2,1)} %bitcast.317), calls=%async_computation.2 | async-start | bytes 3145728 | tf_op jit(solution)/shard_map/all_to_all | solution.py:229
  453.2 84.2 %all-reduce.2.cloned.1.call-start = ((), (), s32[]{:S(2)}) async-start(), calls=%async_computation.4 | async-start | bytes 1572864 | tf_op jit(solution)/shard_map/psum | solution.py:208
  478.9 4.7 copy-start.12
  478.9 76.2 %all-to-all-start.3 = ((bf16[1,4,2,128,768]{4,3,2,0,1:T(8,128)(2,1)}), bf16[1,4,2,128,768]{4,3,2,0,1:T(8,128)(2,1)}, u32[]{:S(2)}, u32[]{:S(2)}) async-start(bf16[1,4,2,128,768]{4,3,2,0,1:T(8,128)(2,1)} %bitcast.318), calls=%async_computation.3 | async-start | bytes 3145728 | tf_op jit(solution)/shard_map/all_to_all | solution.py:230
  487.8 61.8 %copy-start.19 = (s32[8]{0:T(128)S(1)}, s32[8]{0:T(128)}, u32[]{:S(2)}) copy-start(s32[8]{0:T(128)} %copy-done.18) | copy-start | bytes 100
  (23 other events, 63.0 us)
Sparse Core Ops, SparseCore 0:
  461.2 76.1 all-reduce.1
where the time goes:
time: 591 us; the launch traced here: 581 us
  matrix products  248 us (42%)
  local copies, waits for them, and re-layouts  143 us (24%)
  blocking collectives  64 us (11%)
  waiting for transfers between devices  56.5 us (10%)
  other arithmetic  36.8 us (6%)
  starting transfers between devices  18 us (3%)
  between operations  14.7 us (2%)
    dot_general x6, matrix products, group_pass(): jnp.einsum('fhqk,fkhd->fqhd', grad_scores, key_four, preferred_element_ty...  75.5 us
    dot_general x6, matrix products, group_pass(): jnp.einsum('fhqk,fqhd->fkhd', grad_scores, query_four, preferred_element_...  68.3 us
    psum x1, waiting for transfers between devices, local(): whole_grads = lax.psum(total.astype(jnp.bfloat16), 'tm').astype(jnp.float32)  49.6 us
    all_gather x1, blocking collectives, local(): lax.all_gather(kept_keys, 'tm', axis=0, tiled=True)  33 us
    all_gather x1, blocking collectives, local(): lax.all_gather(kept_values, 'tm', axis=0, tiled=True)  30.9 us
    dynamic_slice x24, local copies, waits for them, and re-layouts, local(): lax.map(partial(group_pass, key_live=key_live), (split_groups(queries), s...  24.1 us
    sub x6, matrix products, group_pass(): shifted_exp = jnp.exp(scores - highest)  22.5 us
    unnamed x74, local copies, waits for them, and re-layouts  17.9 us
  transfers between devices with their start and end apart: 5, of which 2 were waited for; matrix products, arithmetic and copies ran while one was open for 14% of the time, Pallas kernels for 0%

commit v1 on v0

v1 whole, which is shorter than its diff:
```python
import functools
import math

import jax
import jax.numpy as jnp
from jax import lax
from jax.experimental import pallas as pl
from jax.experimental.pallas import tpu as pltpu
from jax.sharding import PartitionSpec as P

HDIM = 64
STRIP = 128
MEM = 32
RMAX = 4
EPS = 1e-05
PAIR = 2 * HDIM
WIDE = 2 * PAIR
QB = 256
DEAD = -1e30
SCALE = 1.0 / math.sqrt(HDIM)
MESH = pl.DeviceIdType.MESH
F32 = jnp.float32
BF16 = jnp.bfloat16


def dot(a, b):
    return jnp.dot(a, b, preferred_element_type=F32)


def dot_nt(a, b):
    return lax.dot_general(a, b, (((1,), (1,)), ((), ())), preferred_element_type=F32)


def kernel(
    T,
    C,
    x_hbm,
    wq_hbm,
    wk_hbm,
    wv_hbm,
    wo_hbm,
    gu_hbm,
    off_ref,
    cnt_ref,
    idx_ref,
    upd_hbm,
    gt_hbm,
    x,
    wq,
    wk,
    wv,
    wo,
    gu,
    xn,
    mean_s,
    inv_s,
    kept_mine,
    kept_all,
    mg_send,
    mg_recv,
    kall,
    vall,
    kt_s,
    vt_s,
    bias_s,
    qs,
    gms,
    mixed,
    dq,
    own,
    dk_s,
    dv_s,
    tot,
    gn,
    s_send,
    s_recv,
    b_send,
    b_recv,
    in_sem,
    out_sem,
    kept_ss,
    kept_rs,
    mg_ss,
    mg_rs,
    s_ss,
    s_rs,
    b_ss,
    b_rs,
):
    rows, width = x.shape
    inner = wq.shape[1]
    pairs = inner // PAIR
    reads = off_ref.shape[1]
    slots = idx_ref.shape[2]
    strips = rows // STRIP
    spacing = rows // MEM
    keys = kall.shape[1]
    mem_at = rows
    far_at = rows + reads * MEM
    me = lax.axis_index("tm")
    cam = lax.axis_index("cam")

    loads = [
        pltpu.make_async_copy(src, dst, in_sem.at[i])
        for i, (src, dst) in enumerate(
            [(x_hbm, x), (wk_hbm, wk), (wv_hbm, wv), (wq_hbm, wq), (gu_hbm, gu), (wo_hbm, wo)]
        )
    ]
    for load in loads:
        load.start()

    barrier = pltpu.get_barrier_semaphore()

    def greet(d, carry):
        pl.semaphore_signal(
            barrier, inc=1, device_id=(lax.rem(me + d, T), cam), device_id_type=MESH
        )
        return carry

    lax.fori_loop(1, T, greet, 0)
    for d in range(1, C):
        pl.semaphore_signal(
            barrier, inc=1, device_id=(me, lax.rem(cam + d, C)), device_id_type=MESH
        )

    def kept_copy(d, at, target):
        return pltpu.make_async_remote_copy(
            src_ref=kept_mine,
            dst_ref=kept_all.at[pl.ds(pl.multiple_of(at * MEM, MEM), MEM)],
            send_sem=kept_ss.at[d],
            recv_sem=kept_rs.at[d],
            device_id=(target, cam),
            device_id_type=MESH,
        )

    def mg_copy(d, at, target):
        return pltpu.make_async_remote_copy(
            src_ref=mg_send.at[pl.ds(pl.multiple_of(target * MEM, MEM), MEM)],
            dst_ref=mg_recv.at[pl.ds(pl.multiple_of(at * MEM, MEM), MEM)],
            send_sem=mg_ss.at[d],
            recv_sem=mg_rs.at[d],
            device_id=(target, cam),
            device_id_type=MESH,
        )

    def strip_copy(p, d):
        return pltpu.make_async_remote_copy(
            src_ref=s_send.at[p, d - 1],
            dst_ref=s_recv.at[p, d - 1],
            send_sem=s_ss.at[p, d - 1],
            recv_sem=s_rs.at[p, d - 1],
            device_id=(me, lax.rem(cam + d, C)),
            device_id_type=MESH,
        )

    def back_copy(p, d):
        return pltpu.make_async_remote_copy(
            src_ref=b_send.at[p, d - 1],
            dst_ref=b_recv.at[p, d - 1],
            send_sem=b_ss.at[p, d - 1],
            recv_sem=b_rs.at[p, d - 1],
            device_id=(me, lax.rem(cam + C - d, C)),
            device_id_type=MESH,
        )

    block = 64
    loads[0].wait()

    def norm_step(i, carry):
        at = pl.ds(pl.multiple_of(i * block, block), block)
        wide = x[at, :].astype(F32)
        average = jnp.mean(wide, axis=-1, keepdims=True)
        centred = wide - average
        spread = jnp.mean(centred * centred, axis=-1, keepdims=True)
        inverse = lax.rsqrt(spread + EPS)
        mean_s[at, :] = average
        inv_s[at, :] = inverse
        xn[at, :] = (centred * inverse).astype(BF16)
        return carry

    lax.fori_loop(0, rows // block, norm_step, 0)

    pick = (
        lax.broadcasted_iota(jnp.int32, (MEM, rows), 1)
        == lax.broadcasted_iota(jnp.int32, (MEM, rows), 0) * spacing
    ).astype(F32).astype(BF16)
    kept_x = dot(pick, xn[...]).astype(BF16)
    loads[1].wait()
    loads[2].wait()
    kept_mine[:, :inner] = dot(kept_x, wk[...]).astype(BF16)
    kept_mine[:, inner:] = dot(kept_x, wv[...]).astype(BF16)
    pl.semaphore_wait(barrier, T - 1 + C - 1)

    def kept_start(d, carry):
        @pl.when(me + d < T)
        def _():
            kept_copy(d, me, me + d).start()

        return carry

    lax.fori_loop(1, T, kept_start, 0)

    def kv_step(i, carry):
        cols = pl.ds(pl.multiple_of(i * WIDE, WIDE), WIDE)
        k = dot(xn[...], wk[:, cols]).astype(BF16)
        v = dot(xn[...], wv[:, cols]).astype(BF16)
        for u in range(2):
            p = 2 * i + u
            kall[p, :rows, :] = k[:, u * PAIR : (u + 1) * PAIR]
            vall[p, :rows, :] = v[:, u * PAIR : (u + 1) * PAIR]
        for u in range(2):
            p = 2 * i + u
            for d in range(1, C):
                for t in range(slots):
                    strip = idx_ref[cam, lax.rem(cam + d, C), t]
                    for kv, full in ((0, kall), (1, vall)):
                        part = full[p, :STRIP, :]
                        for n in range(1, strips):
                            part = jnp.where(strip == n, full[p, n * STRIP : (n + 1) * STRIP, :], part)
                        s_send[p, d - 1, t, kv] = part
                strip_copy(p, d).start()
        return carry

    lax.fori_loop(0, pairs // 2, kv_step, 0)

    loads[3].wait()
    loads[4].wait()
    loads[5].wait()

    def q_step(i, carry):
        cols = pl.ds(pl.multiple_of(i * WIDE, WIDE), WIDE)
        q = dot(xn[...], wq[:, cols]).astype(BF16) * jnp.asarray(SCALE, BF16)
        g = dot_nt(gu[...], wo[cols, :]).astype(BF16)
        for u in range(2):
            p = 2 * i + u
            qs[p] = q[:, u * PAIR : (u + 1) * PAIR]
            gms[p] = g[:, u * PAIR : (u + 1) * PAIR]
        return carry

    lax.fori_loop(0, pairs // 2, q_step, 0)

    sources = [me - off_ref[me, j] for j in range(reads)]
    counts = [cnt_ref[lax.rem(cam + C - d, C), cam] for d in range(1, C)]
    position = []
    before = jnp.int32(0)
    for count in counts:
        for t in range(slots):
            position.append(jnp.where(t < count, before + t, -1))
        before = before + count
    lane = lax.broadcasted_iota(jnp.int32, (1, PAIR), 1)
    for h in range(2):
        other = PAIR // 2 if h == 0 else 0
        bias_s[h] = jnp.zeros((keys, PAIR), BF16)
        for j in range(reads):
            level = jnp.where(sources[j] >= 0, 0.0, DEAD).astype(F32)
            part = jnp.where(
                lax.broadcasted_iota(jnp.int32, (MEM, PAIR), 1) == other, level, 0.0
            )
            bias_s[h, mem_at + j * MEM : mem_at + (j + 1) * MEM, :] = part.astype(BF16)
        for r in range(RMAX):
            level = jnp.where(r < before, 0.0, DEAD).astype(F32)
            part = jnp.where(
                lax.broadcasted_iota(jnp.int32, (STRIP, PAIR), 1) == other, level, 0.0
            )
            bias_s[h, far_at + r * STRIP : far_at + (r + 1) * STRIP, :] = part.astype(BF16)

    def zero_step(t, carry):
        mg_recv[pl.ds(pl.multiple_of(t * MEM, MEM), MEM), :] = jnp.zeros((MEM, 2 * inner), BF16)
        return carry

    lax.fori_loop(0, me + 1, zero_step, 0)

    def kept_end(d, carry):
        @pl.when(me - d >= 0)
        def _():
            kept_copy(d, me - d, me).wait_recv()

        return carry

    lax.fori_loop(1, T, kept_end, 0)
    for p in range(pairs):
        for full in (kall, vall):
            full[p, mem_at:far_at, :] = jnp.zeros((reads * MEM, PAIR), BF16)

    def read_step(g, carry):
        part = kept_all[pl.ds(pl.multiple_of(g * MEM, MEM), MEM), :]
        for j in range(reads):
            hit = sources[j] == g
            at = slice(mem_at + j * MEM, mem_at + (j + 1) * MEM)
            for p in range(pairs):
                for first, full in ((0, kall), (inner, vall)):
                    new = part[:, first + p * PAIR : first + (p + 1) * PAIR]
                    full[p, at, :] = jnp.where(hit, new, full[p, at, :])
        return carry

    lax.fori_loop(0, me, read_step, 0)

    def pair_step(p, carry):
        for d in range(1, C):
            strip_copy(p, d).wait_recv()
        for kv, full in ((0, kall), (1, vall)):
            got = [s_recv[p, d, t, kv] for d in range(C - 1) for t in range(slots)]
            for r in range(RMAX):
                part = got[0]
                for s in range(1, len(got)):
                    part = jnp.where(position[s] == r, got[s], part)
                full[p, far_at + r * STRIP : far_at + (r + 1) * STRIP, :] = part
        k_pair = kall[p]
        v_pair = vall[p]
        kt_s[...] = (k_pair.astype(F32) * SCALE).T.astype(BF16)
        vt_s[...] = v_pair.astype(F32).T.astype(BF16)
        in_head = [lane < HDIM, lane >= HDIM]
        zero = jnp.zeros((), BF16)
        mixed_t = [[None] * (rows // QB) for _ in range(2)]
        dq_t = [[None] * (rows // QB) for _ in range(2)]
        for b in range(rows // QB):
            q_blk = qs[p, b * QB : (b + 1) * QB, :]
            g_blk = gms[p, b * QB : (b + 1) * QB, :]
            for h in range(2):
                one = (lane == (HDIM if h == 0 else 0)).astype(F32).astype(BF16)
                k_h = jnp.where(in_head[h], k_pair, bias_s[h])
                v_h = jnp.where(in_head[h], v_pair, zero)
                q_one = jnp.where(in_head[h], q_blk, one)
                q_h = jnp.where(in_head[h], q_blk, zero)
                g_h = jnp.where(in_head[h], g_blk, zero)
                scores = dot_nt(k_h, q_one)
                highest = jnp.max(scores, axis=0, keepdims=True)
                lifted = jnp.exp(scores - highest)
                total = jnp.sum(lifted, axis=0, keepdims=True)
                weights = lifted * (1.0 / total)
                low = weights.astype(BF16)
                grad_w = dot_nt(v_h, g_blk)
                inner_sum = jnp.sum(weights * grad_w, axis=0, keepdims=True)
                grad_s = (weights * (grad_w - inner_sum)).astype(BF16)
                mixed_t[h][b] = dot(vt_s[h * HDIM : (h + 1) * HDIM, :], low)
                dq_t[h][b] = dot(kt_s[h * HDIM : (h + 1) * HDIM, :], grad_s)
                dv = dot(low, g_h)
                dk = dot(grad_s, q_h)
                if b == 0 and h == 0:
                    dv_s[...] = dv
                    dk_s[...] = dk
                else:
                    dv_s[...] += dv
                    dk_s[...] += dk
            cols = pl.ds(pl.multiple_of(p * PAIR, PAIR), PAIR)
            at = slice(b * QB, (b + 1) * QB)
            mixed[at, cols] = jnp.concatenate([mixed_t[0][b], mixed_t[1][b]], axis=0).T.astype(BF16)
            dq[at, cols] = jnp.concatenate([dq_t[0][b], dq_t[1][b]], axis=0).T.astype(BF16)
        for kv, grads in ((0, dk_s), (1, dv_s)):
            own[kv, p] = grads[:rows, :]
            cols = pl.ds(pl.multiple_of(kv * inner + p * PAIR, PAIR), PAIR)

            def mem_step(g, carry, grads=grads, cols=cols):
                part = jnp.zeros((MEM, PAIR), F32)
                for j in range(reads):
                    read = grads[mem_at + j * MEM : mem_at + (j + 1) * MEM, :]
                    part = part + jnp.where(sources[j] == g, read, 0.0)
                mg_send[pl.ds(pl.multiple_of(g * MEM, MEM), MEM), cols] = part.astype(BF16)
                return carry

            lax.fori_loop(0, T, mem_step, 0)
            far = [
                grads[far_at + r * STRIP : far_at + (r + 1) * STRIP, :].astype(BF16)
                for r in range(RMAX)
            ]
            for s in range((C - 1) * slots):
                part = jnp.zeros((STRIP, PAIR), BF16)
                for r in range(RMAX):
                    part = jnp.where(position[s] == r, far[r], part)
                b_send[p, s // slots, s % slots, kv] = part
        for d in range(1, C):
            back_copy(p, d).start()
        return carry

    lax.fori_loop(0, pairs, pair_step, 0)

    def mg_start(d, carry):
        @pl.when(me - d >= 0)
        def _():
            mg_copy(d, me, me - d).start()

        return carry

    lax.fori_loop(1, T, mg_start, 0)

    def update_step(i, carry):
        cols = pl.ds(pl.multiple_of(i * WIDE, WIDE), WIDE)
        gu[:, cols] = dot(mixed[...], wo[:, cols]).astype(BF16)
        gn[:, cols] = dot_nt(dq[...], wq[cols, :])
        return carry

    lax.fori_loop(0, width // WIDE, update_step, 0)
    update_out = pltpu.make_async_copy(gu, upd_hbm, out_sem.at[0])
    update_out.start()

    def mg_end(d, carry):
        @pl.when(me + d < T)
        def _():
            mg_copy(d, me + d, me).wait_recv()

        return carry

    lax.fori_loop(1, T, mg_end, 0)
    place = (
        lax.broadcasted_iota(jnp.int32, (rows, T * MEM), 0)
        == lax.rem(lax.broadcasted_iota(jnp.int32, (rows, T * MEM), 1), MEM) * spacing
    ).astype(F32).astype(BF16)

    def total_step(p, carry):
        for d in range(1, C):
            back_copy(p, d).wait_recv()
        for kv in range(2):
            cols = pl.ds(pl.multiple_of(kv * inner + p * PAIR, PAIR), PAIR)
            grown = own[kv, p] + dot(place, mg_recv[:, cols])
            for n in range(strips):
                part = grown[n * STRIP : (n + 1) * STRIP, :]
                for d in range(1, C):
                    came = jnp.zeros((STRIP, PAIR), BF16)
                    for t in range(slots):
                        hit = idx_ref[cam, lax.rem(cam + d, C), t] == n
                        came = jnp.where(hit, b_recv[p, d - 1, t, kv], came)
                    part = part + came.astype(F32)
                tot[n * STRIP : (n + 1) * STRIP, cols] = part.astype(BF16)
        return carry

    lax.fori_loop(0, pairs, total_step, 0)

    def grad_step(i, carry):
        cols = pl.ds(pl.multiple_of(i * WIDE, WIDE), WIDE)
        gn[:, cols] += dot_nt(tot[:, :inner], wk[cols, :]) + dot_nt(tot[:, inner:], wv[cols, :])
        return carry

    lax.fori_loop(0, width // WIDE, grad_step, 0)

    def back_norm_step(i, carry):
        at = pl.ds(pl.multiple_of(i * block, block), block)
        inverse = inv_s[at, :]
        normed = (x[at, :].astype(F32) - mean_s[at, :]) * inverse
        grads = gn[at, :]
        first = jnp.mean(grads, axis=-1, keepdims=True)
        second = jnp.mean(grads * normed, axis=-1, keepdims=True)
        xn[at, :] = (inverse * (grads - first - normed * second)).astype(BF16)
        return carry

    lax.fori_loop(0, rows // block, back_norm_step, 0)
    grad_out = pltpu.make_async_copy(xn, gt_hbm, out_sem.at[1])
    grad_out.start()

    def sent_step(d, carry):
        @pl.when(me + d < T)
        def _():
            kept_copy(d, me, me + d).wait_send()

        @pl.when(me - d >= 0)
        def _():
            mg_copy(d, me, me - d).wait_send()

        return carry

    lax.fori_loop(1, T, sent_step, 0)

    def sent_strip_step(p, carry):
        for d in range(1, C):
            strip_copy(p, d).wait_send()
            back_copy(p, d).wait_send()
        return carry

    lax.fori_loop(0, pairs, sent_strip_step, 0)
    update_out.wait()
    grad_out.wait()


def local(
    T,
    C,
    tokens,
    w_query,
    w_key,
    w_value,
    w_out,
    grad_update,
    memory_offsets,
    strip_count,
    strip_index,
):
    rows, width = tokens.shape[2:]
    inner = w_query.shape[1]
    pairs = inner // PAIR
    reads = memory_offsets.shape[1]
    slots = strip_index.shape[2]
    keys = rows + reads * MEM + RMAX * STRIP
    vmem = pltpu.VMEM
    hbm = pl.BlockSpec(memory_space=pl.ANY)
    smem = pl.BlockSpec(memory_space=pltpu.SMEM)
    strip_shape = (pairs, C - 1, slots, 2, STRIP, PAIR)
    dma = pltpu.SemaphoreType.DMA
    update, grad_tokens = pl.pallas_call(
        functools.partial(kernel, T, C),
        out_shape=[jax.ShapeDtypeStruct((rows, width), BF16)] * 2,
        in_specs=[hbm] * 6 + [smem] * 3,
        out_specs=[hbm] * 2,
        scratch_shapes=[
            vmem((rows, width), BF16),
            vmem((width, inner), BF16),
            vmem((width, inner), BF16),
            vmem((width, inner), BF16),
            vmem((inner, width), BF16),
            vmem((rows, width), BF16),
            vmem((rows, width), BF16),
            vmem((rows, 1), F32),
            vmem((rows, 1), F32),
            vmem((MEM, 2 * inner), BF16),
            vmem((T * MEM, 2 * inner), BF16),
            vmem((T * MEM, 2 * inner), BF16),
            vmem((T * MEM, 2 * inner), BF16),
            vmem((pairs, keys, PAIR), BF16),
            vmem((pairs, keys, PAIR), BF16),
            vmem((PAIR, keys), BF16),
            vmem((PAIR, keys), BF16),
            vmem((2, keys, PAIR), BF16),
            vmem((pairs, rows, PAIR), BF16),
            vmem((pairs, rows, PAIR), BF16),
            vmem((rows, inner), BF16),
            vmem((rows, inner), BF16),
            vmem((2, pairs, rows, PAIR), F32),
            vmem((keys, PAIR), F32),
            vmem((keys, PAIR), F32),
            vmem((rows, 2 * inner), BF16),
            vmem((rows, width), F32),
            vmem(strip_shape, BF16),
            vmem(strip_shape, BF16),
            vmem(strip_shape, BF16),
            vmem(strip_shape, BF16),
            dma((6,)),
            dma((2,)),
            dma((T,)),
            dma((T,)),
            dma((T,)),
            dma((T,)),
            dma((pairs, C - 1)),
            dma((pairs, C - 1)),
            dma((pairs, C - 1)),
            dma((pairs, C - 1)),
        ],
        compiler_params=pltpu.CompilerParams(
            collective_id=0, has_side_effects=True, vmem_limit_bytes=60 * 1024 * 1024
        ),
    )(
        tokens.reshape(rows, width),
        w_query,
        w_key,
        w_value,
        w_out,
        grad_update.reshape(rows, width),
        memory_offsets,
        strip_count,
        strip_index,
    )
    return update.reshape(1, 1, rows, width), grad_tokens.reshape(1, 1, rows, width)


def solution(mesh):
    split = P("cam", "tm", None, None)
    in_specs = (split, P(), P(), P(), P(), split, P(), P(), P())
    return jax.shard_map(
        functools.partial(local, mesh.shape["tm"], mesh.shape["cam"]),
        mesh=mesh,
        in_specs=in_specs,
        out_specs=(split, split),
        check_vma=False,
    )
```

time: 591 us -> 97.7 us (0.17); the launches traced: 581 us -> 97.5 us
  matrix products: 248 us -> 0 us
  local copies, waits for them, and re-layouts: 143 us -> 6.65 us
  Pallas kernels: 0 us -> 90.2 us
  blocking collectives: 64 us -> 0 us
  waiting for transfers between devices: 56.5 us -> 0 us
  other arithmetic: 36.8 us -> 0 us
  starting transfers between devices: 18 us -> 0 us
  between operations: 14.7 us -> 0.65 us
    dot_general x42 -> x0, matrix products: 225 us -> none  [the longest x6 75.5 us: group_pass(): jnp.einsum('fhqk,fkhd->fqhd', grad_scores, key_four, preferred_element_ty...]
    pallas_call x0 -> x1, Pallas kernels: none -> 90.2 us  [local(): pl.pallas_call(functools.partial(kernel, T, C), out_shape=[jax.ShapeDtype...]
    all_gather x2 -> x0, blocking collectives: 64 us -> none  [the longest x1 33 us: local(): lax.all_gather(kept_keys, 'tm', axis=0, tiled=True)]
    psum x1 -> x0, waiting for transfers between devices: 49.6 us -> none  [local(): whole_grads = lax.psum(total.astype(jnp.bfloat16), 'tm').astype(jnp.float32)]
    dynamic_slice x27 -> x0, local copies, waits for them, and re-layouts: 25.9 us -> none  [the longest x24 24.1 us: local(): lax.map(partial(group_pass, key_live=key_live), (split_groups(queries), s...]
    slice x16 -> x0, local copies, waits for them, and re-layouts: 23.5 us -> none  [the longest x2 5.82 us: local(): grad_keys_all[:, :row_count].reshape(frames_here, MEM, spacing, inner_width)]
    gather x6 -> x0, local copies, waits for them, and re-layouts: 23.1 us -> none  [the longest x1 13.7 us: local(): jnp.take(far_grad_keys.reshape(frames_here, RMAX, STRIP * inner_width), s...]
    sub x6 -> x0, matrix products: 22.5 us -> none  [group_pass(): shifted_exp = jnp.exp(scores - highest)]
  transfers between devices with their start and end apart: 5 -> 0, of which waited for: 2 -> 0; matrix products, arithmetic and copies ran while one was open for 14% -> 0% of each run, Pallas kernels for 0% -> 0%
where the time goes in v1:
time: 97.7 us; the launch traced here: 97.5 us
  Pallas kernels  90.2 us (92%)
  local copies, waits for them, and re-layouts  6.65 us (7%)
    pallas_call x1, Pallas kernels, local(): pl.pallas_call(functools.partial(kernel, T, C), out_shape=[jax.ShapeDtype...  90.2 us
    unnamed x6, local copies, waits for them, and re-layouts  6.65 us

profile of v1, /device:TPU:0, one launch (start us, length us, event | category | flops | bytes accessed | tf_op | source)
XLA Modules:
  0.0 97.5 jit_solution(16252632595084231434)
XLA Ops:
  0.6 1.3 %copy.11.off_ref = s32[8,4]{1,0:T(8,128)} copy(s32[8,4]{0,1:T(4,128)} %param.15) | data formatting | bytes 256 | tf_op args[6]
  2.0 1.4 %copy.12.idx_ref = s32[4,4,2]{2,1,0:T(4,128)} copy(s32[4,4,2]{1,2,0:T(2,128)} %param.17) | data formatting | bytes 256 | tf_op args[8]
  3.4 90.2 %shard_map.104 = (bf16[512,1536]{1,0:T(8,128)(2,1)}, bf16[512,1536]{1,0:T(8,128)(2,1)}) custom-call(bf16[512,1536]{1,0:T(8,128)(2,1)} %bitcast.6, bf16[1536,768]{1,0:T(8,128)(2,1)} %wq_hbm.1, bf16[1536,768]{1,0:T(8,128)(2,1)} %wk_hbm.1, bf16[1536,768]{1,0:T(8,128)(2,1)} %wv_hbm.1, bf16[768,1536]{1,0:T(8,128)(2,1)} %wo_hbm.1, bf16[512,1536]{1,0:T(8,128)(2,1)} %bitcast.7, ...), custom_call_target="tpu_custom_call" | custom-call | tf_op jit(solution)/shard_map/pallas_call | solution.py:497
  93.5 0.0 copy-start
  93.5 2.8 %copy.15 = bf16[1,1,512,1536]{3,2,1,0:T(8,128)(2,1)} copy(bf16[1,1,512,1536]{3,2,1,0:T(8,128)(2,1)} %bitcast.5) | data formatting | bytes 3145728
  96.3 0.0 copy-done
  96.3 1.1 %copy.16 = bf16[1,1,512,1536]{3,2,1,0:T(8,128)(2,1)} copy(bf16[1,1,512,1536]{3,2,1,0:T(8,128)(2,1)S(1)} %bitcast.4) | data formatting | bytes 3145728
Async XLA Ops:
  93.5 2.8 %copy-start = (bf16[512,1536]{1,0:T(8,128)(2,1)S(1)}, bf16[512,1536]{1,0:T(8,128)(2,1)}, u32[]{:S(2)}) copy-start(bf16[512,1536]{1,0:T(8,128)(2,1)} %get-tuple-element.5) | copy-start | bytes 4718596

commit v2 on v1

--- a/solution.py
+++ b/solution.py
@@ -90,6 +90,7 @@
     rows, width = x.shape
     inner = wq.shape[1]
     pairs = inner // PAIR
+    groups = pairs // 2
     reads = off_ref.shape[1]
     slots = idx_ref.shape[2]
     strips = rows // STRIP
@@ -123,22 +124,25 @@
             barrier, inc=1, device_id=(me, lax.rem(cam + d, C)), device_id_type=MESH
         )
 
-    def kept_copy(d, at, target):
+    def slab(at):
+        return pl.ds(pl.multiple_of(at * MEM, MEM), MEM)
+
+    def kept_copy(i, d, at, target):
         return pltpu.make_async_remote_copy(
-            src_ref=kept_mine,
-            dst_ref=kept_all.at[pl.ds(pl.multiple_of(at * MEM, MEM), MEM)],
-            send_sem=kept_ss.at[d],
-            recv_sem=kept_rs.at[d],
+            src_ref=kept_mine.at[i],
+            dst_ref=kept_all.at[i, slab(at)],
+            send_sem=kept_ss.at[i, d],
+            recv_sem=kept_rs.at[i, d],
             device_id=(target, cam),
             device_id_type=MESH,
         )
 
-    def mg_copy(d, at, target):
+    def mg_copy(i, d, at, target):
         return pltpu.make_async_remote_copy(
-            src_ref=mg_send.at[pl.ds(pl.multiple_of(target * MEM, MEM), MEM)],
-            dst_ref=mg_recv.at[pl.ds(pl.multiple_of(at * MEM, MEM), MEM)],
-            send_sem=mg_ss.at[d],
-            recv_sem=mg_rs.at[d],
+            src_ref=mg_send.at[i, slab(target)],
+            dst_ref=mg_recv.at[i, slab(at)],
+            send_sem=mg_ss.at[i, d],
+            recv_sem=mg_rs.at[i, d],
             device_id=(target, cam),
             device_id_type=MESH,
         )
@@ -187,18 +191,22 @@
     kept_x = dot(pick, xn[...]).astype(BF16)
     loads[1].wait()
     loads[2].wait()
-    kept_mine[:, :inner] = dot(kept_x, wk[...]).astype(BF16)
-    kept_mine[:, inner:] = dot(kept_x, wv[...]).astype(BF16)
+    for first, weight in ((0, wk), (WIDE, wv)):
+        kept = dot(kept_x, weight[...]).astype(BF16)
+        for i in range(groups):
+            kept_mine[i, :, first : first + WIDE] = kept[:, i * WIDE : (i + 1) * WIDE]
     pl.semaphore_wait(barrier, T - 1 + C - 1)
 
-    def kept_start(d, carry):
-        @pl.when(me + d < T)
-        def _():
-            kept_copy(d, me, me + d).start()
-
-        return carry
-
-    lax.fori_loop(1, T, kept_start, 0)
+    for i in range(groups):
+
+        def kept_start(d, carry, i=i):
+            @pl.when(me + d < T)
+            def _():
+                kept_copy(i, d, me, me + d).start()
+
+            return carry
+
+        lax.fori_loop(1, T, kept_start, 0)
 
     def kv_step(i, carry):
         cols = pl.ds(pl.multiple_of(i * WIDE, WIDE), WIDE)
@@ -265,37 +273,47 @@
             bias_s[h, far_at + r * STRIP : far_at + (r + 1) * STRIP, :] = part.astype(BF16)
 
     def zero_step(t, carry):
-        mg_recv[pl.ds(pl.multiple_of(t * MEM, MEM), MEM), :] = jnp.zeros((MEM, 2 * inner), BF16)
+        for i in range(groups):
+            mg_recv[i, slab(t), :] = jnp.zeros((MEM, 2 * WIDE), BF16)
         return carry
 
     lax.fori_loop(0, me + 1, zero_step, 0)
 
-    def kept_end(d, carry):
-        @pl.when(me - d >= 0)
-        def _():
-            kept_copy(d, me - d, me).wait_recv()
-
-        return carry
-
-    lax.fori_loop(1, T, kept_end, 0)
     for p in range(pairs):
         for full in (kall, vall):
             full[p, mem_at:far_at, :] = jnp.zeros((reads * MEM, PAIR), BF16)
 
-    def read_step(g, carry):
-        part = kept_all[pl.ds(pl.multiple_of(g * MEM, MEM), MEM), :]
-        for j in range(reads):
-            hit = sources[j] == g
-            at = slice(mem_at + j * MEM, mem_at + (j + 1) * MEM)
-            for p in range(pairs):
-                for first, full in ((0, kall), (inner, vall)):
-                    new = part[:, first + p * PAIR : first + (p + 1) * PAIR]
-                    full[p, at, :] = jnp.where(hit, new, full[p, at, :])
-        return carry
-
-    lax.fori_loop(0, me, read_step, 0)
+    def read_group(i):
+        def kept_end(d, carry):
+            @pl.when(me - d >= 0)
+            def _():
+                kept_copy(i, d, me - d, me).wait_recv()
+
+            return carry
+
+        lax.fori_loop(1, T, kept_end, 0)
+
+        def read_step(g, carry):
+            part = kept_all[i, slab(g), :]
+            for j in range(reads):
+                hit = sources[j] == g
+                at = slice(mem_at + j * MEM, mem_at + (j + 1) * MEM)
+                for u in range(2):
+                    for first, full in ((0, kall), (WIDE, vall)):
+                        new = part[:, first + u * PAIR : first + (u + 1) * PAIR]
+                        full[2 * i + u, at, :] = jnp.where(hit, new, full[2 * i + u, at, :])
+            return carry
+
+        lax.fori_loop(0, me, read_step, 0)
 
     def pair_step(p, carry):
+        group = lax.div(p, 2)
+        half = lax.rem(p, 2)
+
+        @pl.when(half == 0)
+        def _():
+            read_group(group)
+
         for d in range(1, C):
             strip_copy(p, d).wait_recv()
         for kv, full in ((0, kall), (1, vall)):
@@ -348,14 +366,14 @@
             dq[at, cols] = jnp.concatenate([dq_t[0][b], dq_t[1][b]], axis=0).T.astype(BF16)
         for kv, grads in ((0, dk_s), (1, dv_s)):
             own[kv, p] = grads[:rows, :]
-            cols = pl.ds(pl.multiple_of(kv * inner + p * PAIR, PAIR), PAIR)
+            cols = pl.ds(pl.multiple_of(kv * WIDE + half * PAIR, PAIR), PAIR)
 
             def mem_step(g, carry, grads=grads, cols=cols):
                 part = jnp.zeros((MEM, PAIR), F32)
                 for j in range(reads):
                     read = grads[mem_at + j * MEM : mem_at + (j + 1) * MEM, :]
                     part = part + jnp.where(sources[j] == g, read, 0.0)
-                mg_send[pl.ds(pl.multiple_of(g * MEM, MEM), MEM), cols] = part.astype(BF16)
+                mg_send[group, slab(g), cols] = part.astype(BF16)
                 return carry
 
             lax.fori_loop(0, T, mem_step, 0)
@@ -370,18 +388,21 @@
                 b_send[p, s // slots, s % slots, kv] = part
         for d in range(1, C):
             back_copy(p, d).start()
+
+        @pl.when(half == 1)
+        def _():
+            def mg_start(d, carry):
+                @pl.when(me - d >= 0)
+                def _():
+                    mg_copy(group, d, me, me - d).start()
+
+                return carry
+
+            lax.fori_loop(1, T, mg_start, 0)
+
         return carry
 
     lax.fori_loop(0, pairs, pair_step, 0)
-
-    def mg_start(d, carry):
-        @pl.when(me - d >= 0)
-        def _():
-            mg_copy(d, me, me - d).start()
-
-        return carry
-
-    lax.fori_loop(1, T, mg_start, 0)
 
     def update_step(i, carry):
         cols = pl.ds(pl.multiple_of(i * WIDE, WIDE), WIDE)
@@ -393,25 +414,32 @@
     update_out = pltpu.make_async_copy(gu, upd_hbm, out_sem.at[0])
     update_out.start()
 
-    def mg_end(d, carry):
-        @pl.when(me + d < T)
-        def _():
-            mg_copy(d, me + d, me).wait_recv()
-
-        return carry
-
-    lax.fori_loop(1, T, mg_end, 0)
     place = (
         lax.broadcasted_iota(jnp.int32, (rows, T * MEM), 0)
         == lax.rem(lax.broadcasted_iota(jnp.int32, (rows, T * MEM), 1), MEM) * spacing
     ).astype(F32).astype(BF16)
 
     def total_step(p, carry):
+        group = lax.div(p, 2)
+        half = lax.rem(p, 2)
+
+        @pl.when(half == 0)
+        def _():
+            def mg_end(d, carry):
+                @pl.when(me + d < T)
+                def _():
+                    mg_copy(group, d, me + d, me).wait_recv()
+
+                return carry
+
+            lax.fori_loop(1, T, mg_end, 0)
+
         for d in range(1, C):
             back_copy(p, d).wait_recv()
         for kv in range(2):
             cols = pl.ds(pl.multiple_of(kv * inner + p * PAIR, PAIR), PAIR)
-            grown = own[kv, p] + dot(place, mg_recv[:, cols])
+            came_at = pl.ds(pl.multiple_of(kv * WIDE + half * PAIR, PAIR), PAIR)
+            grown = own[kv, p] + dot(place, mg_recv[group, :, came_at])
             for n in range(strips):
                 part = grown[n * STRIP : (n + 1) * STRIP, :]
                 for d in range(1, C):
@@ -449,11 +477,13 @@
     def sent_step(d, carry):
         @pl.when(me + d < T)
         def _():
-            kept_copy(d, me, me + d).wait_send()
+            for i in range(groups):
+                kept_copy(i, d, me, me + d).wait_send()
 
         @pl.when(me - d >= 0)
         def _():
-            mg_copy(d, me, me - d).wait_send()
+            for i in range(groups):
+                mg_copy(i, d, me, me - d).wait_send()
 
         return carry
 
@@ -509,10 +539,10 @@
             vmem((rows, width), BF16),
             vmem((rows, 1), F32),
             vmem((rows, 1), F32),
-            vmem((MEM, 2 * inner), BF16),
-            vmem((T * MEM, 2 * inner), BF16),
-            vmem((T * MEM, 2 * inner), BF16),
-            vmem((T * MEM, 2 * inner), BF16),
+            vmem((pairs // 2, MEM, 2 * WIDE), BF16),
+            vmem((pairs // 2, T * MEM, 2 * WIDE), BF16),
+            vmem((pairs // 2, T * MEM, 2 * WIDE), BF16),
+            vmem((pairs // 2, T * MEM, 2 * WIDE), BF16),
             vmem((pairs, keys, PAIR), BF16),
             vmem((pairs, keys, PAIR), BF16),
             vmem((PAIR, keys), BF16),
@@ -533,10 +563,10 @@
             vmem(strip_shape, BF16),
             dma((6,)),
             dma((2,)),
-            dma((T,)),
-            dma((T,)),
-            dma((T,)),
-            dma((T,)),
+            dma((pairs // 2, T)),
+            dma((pairs // 2, T)),
+            dma((pairs // 2, T)),
+            dma((pairs // 2, T)),
             dma((pairs, C - 1)),
             dma((pairs, C - 1)),
             dma((pairs, C - 1)),

time: 97.7 us -> 93.9 us (0.961)
  Pallas kernels: 90.2 us -> 86.3 us
    pallas_call x1, Pallas kernels: 90.2 us -> 86.3 us  [local(): pl.pallas_call(functools.partial(kernel, T, C), out_shape=[jax.ShapeDtype...]
where the time goes in v2:
time: 93.9 us; the launch traced here: 93.6 us
  Pallas kernels  86.3 us (92%)
  local copies, waits for them, and re-layouts  6.65 us (7%)
    pallas_call x1, Pallas kernels, local(): pl.pallas_call(functools.partial(kernel, T, C), out_shape=[jax.ShapeDtype...  86.3 us
    unnamed x6, local copies, waits for them, and re-layouts  6.65 us

profile of v2, /device:TPU:0, one launch (start us, length us, event | category | flops | bytes accessed | tf_op | source)
XLA Modules:
  0.0 93.6 jit_solution(18280295021285084569)
XLA Ops:
  0.6 1.3 %copy.11.off_ref = s32[8,4]{1,0:T(8,128)} copy(s32[8,4]{0,1:T(4,128)} %param.15) | data formatting | bytes 256 | tf_op args[6]
  2.0 1.4 %copy.12.idx_ref = s32[4,4,2]{2,1,0:T(4,128)} copy(s32[4,4,2]{1,2,0:T(2,128)} %param.17) | data formatting | bytes 256 | tf_op args[8]
  3.4 86.3 %shard_map.104 = (bf16[512,1536]{1,0:T(8,128)(2,1)}, bf16[512,1536]{1,0:T(8,128)(2,1)}) custom-call(bf16[512,1536]{1,0:T(8,128)(2,1)} %bitcast.6, bf16[1536,768]{1,0:T(8,128)(2,1)} %wq_hbm.1, bf16[1536,768]{1,0:T(8,128)(2,1)} %wk_hbm.1, bf16[1536,768]{1,0:T(8,128)(2,1)} %wv_hbm.1, bf16[768,1536]{1,0:T(8,128)(2,1)} %wo_hbm.1, bf16[512,1536]{1,0:T(8,128)(2,1)} %bitcast.7, ...), custom_call_target="tpu_custom_call" | custom-call | tf_op jit(solution)/shard_map/pallas_call | solution.py:527
  89.7 0.0 copy-start
  89.7 2.8 %copy.15 = bf16[1,1,512,1536]{3,2,1,0:T(8,128)(2,1)} copy(bf16[1,1,512,1536]{3,2,1,0:T(8,128)(2,1)} %bitcast.5) | data formatting | bytes 3145728
  92.4 0.0 copy-done
  92.5 1.1 %copy.16 = bf16[1,1,512,1536]{3,2,1,0:T(8,128)(2,1)} copy(bf16[1,1,512,1536]{3,2,1,0:T(8,128)(2,1)S(1)} %bitcast.4) | data formatting | bytes 3145728
Async XLA Ops:
  89.7 2.8 %copy-start = (bf16[512,1536]{1,0:T(8,128)(2,1)S(1)}, bf16[512,1536]{1,0:T(8,128)(2,1)}, u32[]{:S(2)}) copy-start(bf16[512,1536]{1,0:T(8,128)(2,1)} %get-tuple-element.5) | copy-start | bytes 4718596
